TPU v7x, 32 devices: a whole 2x2x4 slice. The times are simulated.
32 devices in a mesh: row: 4 (over y, x), col: 8 (over z, core).
Axes of the slice: x: 2, y: 2, z: 4, core: 2. Of those that a mesh axis runs over, the one named last changes fastest.
Arguments:
- x_feats: bfloat16 [4096, 128], P(('col', 'row')), may hold values from -6 to 6
- weight: bfloat16 [128, 128], replicated, may hold values from -0.5 to 0.5
- bias: float32 [128], replicated, may hold values from -3 to 3
- block_values: bfloat16 [4, 8, 192, 128, 128], P('row', 'col'), may hold values from -0.0546875 to 0.0546875
- block_rows: int32 [4, 8, 192], P('row', 'col'), may hold values from 0 to 31, as said below
- block_cols: int32 [4, 8, 192], P('row', 'col'), may hold values from 0 to 31, as said below
- block_counts: int32 [4, 8], P('row', 'col'), may hold values from 2 to 192, as said below
- cotangent: bfloat16 [4096, 128], P(('col', 'row')), may hold values from -0.09375 to 0.09375
Outputs:
- activations: bfloat16 [4096, 128], P(('col', 'row'))
- weight_grad: float32 [128, 128], replicated
- bias_grad: float32 [128], replicated
Inputs may be any that keep to these rules, and one draw needn't show every extreme that they name: `block_rows`: grid cell (r, c) owns node segment c * 4 + r, the nodes c * 4 * 128 + r * 128 onward. Every slot of cell (r, c), used or not, names a row block inside a segment s with s % 4 == r and a column block inside a segment t with t // 4 == c, and the row block is at most the column block. Pairs may repeat. `block_cols`: see block_rows. `block_counts`: every cell uses at least 2 slots; some cell uses all 192 slots.
All inputs are finite; a program needn't handle non-finite values.
Results may differ from a plain program's by a relative error of at most 0.008.
Values may be sent and summed in bfloat16 or wider, within the bound.
A program may use at most 128 MiB of HBM per device.

v0:
```python
import jax
import jax.numpy as jnp
from jax import lax
from jax.sharding import PartitionSpec as P


def gelu_parts(pre):
    cdf = 0.5 * (1.0 + lax.erf(pre * 0.7071067811865476))
    dens = jnp.exp(-0.5 * pre * pre) * 0.3989422804014327
    return (pre * cdf, cdf + pre * dens)


def aggregate(feats, matrices, row_slot, col_slot, group_rows, group_cols):
    width = feats.shape[1]
    block = matrices.shape[-1]
    col_side = lax.all_gather(feats, "row", axis=0, tiled=True).reshape(-1, block, width)
    row_side = lax.all_gather(feats, "col", axis=0, tiled=True).reshape(-1, block, width)
    forward_terms = jnp.einsum(
        "kab,kbw->kaw", matrices, col_side[col_slot], preferred_element_type=jnp.float32
    )
    mirror_terms = jnp.einsum(
        "kba,kbw->kaw", matrices, row_side[row_slot], preferred_element_type=jnp.float32
    )
    row_sums = jax.ops.segment_sum(forward_terms, row_slot, num_segments=group_rows)
    col_sums = jax.ops.segment_sum(mirror_terms, col_slot, num_segments=group_cols)
    row_part = lax.psum_scatter(row_sums.reshape(-1, width), "col", scatter_dimension=0, tiled=True)
    col_part = lax.psum_scatter(col_sums.reshape(-1, width), "row", scatter_dimension=0, tiled=True)
    return row_part + col_part


def on_device(x_feats, weight, bias, block_values, block_rows, block_cols, block_counts, cotangent):
    block = block_values.shape[-1]
    per_seg = x_feats.shape[0] // block
    grid_rows = lax.axis_size("row")
    grid_cols = lax.axis_size("col")
    slots = block_values.shape[2]
    used = jnp.arange(slots) < block_counts[0, 0]
    matrices = jnp.where(used[:, None, None], block_values[0, 0], jnp.zeros((), jnp.bfloat16))
    rows_id = block_rows[0, 0]
    cols_id = block_cols[0, 0]
    row_slot = rows_id // per_seg // grid_rows * per_seg + rows_id % per_seg
    col_slot = cols_id // per_seg % grid_rows * per_seg + cols_id % per_seg
    group_rows = grid_cols * per_seg
    group_cols = grid_rows * per_seg
    hidden = jnp.dot(x_feats, weight, preferred_element_type=jnp.float32).astype(jnp.bfloat16)
    pre = aggregate(hidden, matrices, row_slot, col_slot, group_rows, group_cols) + bias
    act, slope = gelu_parts(pre)
    grad_pre = (cotangent.astype(jnp.float32) * slope).astype(jnp.bfloat16)
    back = aggregate(grad_pre, matrices, row_slot, col_slot, group_rows, group_cols)
    local_weight = jnp.dot(x_feats.astype(jnp.float32).T, back, precision=lax.Precision.HIGHEST)
    local_bias = jnp.sum(grad_pre.astype(jnp.float32), axis=0)
    weight_grad, bias_grad = lax.psum((local_weight, local_bias), ("row", "col"))
    return (act.astype(jnp.bfloat16), weight_grad, bias_grad)


def solution(mesh):
    in_specs = (
        P(("col", "row"), None),
        P(),
        P(),
        P("row", "col", None, None, None),
        P("row", "col", None),
        P("row", "col", None),
        P("row", "col"),
        P(("col", "row"), None),
    )
    out_specs = (P(("col", "row"), None), P(), P())
    return jax.shard_map(
        on_device, mesh=mesh, in_specs=in_specs, out_specs=out_specs, check_vma=False
    )
```

profile of v0, /device:TPU:0, one launch (start us, length us, event | category | flops | bytes accessed | tf_op | source)
XLA Modules:
  0.0 430.2 jit_solution(13613128049045931770)
XLA Ops:
  7.2 0.7 compare_select_fusion.1
  8.6 0.7 compare_select_fusion
  9.3 0.9 convolution_convert_fusion
  10.2 15.9 %all_gather.13 = bf16[1024,128]{1,0:T(8,128)(2,1)S(1)} all-gather(bf16[128,128]{1,0:T(8,128)(2,1)S(1)} %convolution_convert_fusion), channel_id=1, replica_groups=mesh['row'=4,'col'=8] {'col'}, dimensions={0}, use_global_device_ids=true | all-gather | bytes 294912 | tf_op jit(solution)/shard_map/all_gather | solution.py:17
  26.1 7.8 %gather_fusion.1 = bf16[192,128,128]{2,1,0:T(8,128)(2,1)} fusion(bf16[8,128,128]{2,1,0:T(8,128)(2,1)S(1)} %bitcast.48, s32[1024]{0:T(1024)S(1)} %pad_clamp_fusion), kind=kCustom, calls=%fused_computation.1 | custom fusion | bytes 12583680 | tf_op jit(solution)/shard_map/gather | solution.py:22
  33.9 11.6 %fusion.10 = f32[192,128,128]{2,1,0:T(8,128)} fusion(bf16[192,128,128]{2,1,0:T(8,128)(2,1)} %gather_fusion.1, bf16[1,1,192,128,128]{4,3,2,1,0:T(8,128)(2,1)} %param.11, pred[192]{0:T(512)(128)(4,1)S(1)} %iota_compare_fusion), kind=kOutput, calls=%fused_computation.39 | convolution fusion | flops 808452096 | bytes 25166016 | tf_op jit(solution)/shard_map/kba,kbw->kaw/dot_general | solution.py:21
  45.5 25.2 %scatter_fusion.1 = f32[4,128,128]{2,1,0:T(8,128)S(1)} fusion(f32[4,128,128]{2,1,0:T(8,128)S(1)} %broadcast.294.clone, s32[192]{0:T(256)S(1)} %bitcast.51, f32[192,128,128]{2,1,0:T(8,128)} %fusion.10), kind=kCustom, calls=%fused_computation.5 | custom fusion | flops 3145728 | bytes 37749504 | tf_op jit(solution)/shard_map/scatter-add | solution.py:25
  70.8 0.7 copy-done.2
  71.5 0.0 reduce-scatter.5.cloned.1.call-start
  71.5 8.6 %all_gather.12 = bf16[512,128]{1,0:T(8,128)(2,1)S(1)} all-gather(bf16[128,128]{1,0:T(8,128)(2,1)S(1)} %convolution_convert_fusion), channel_id=1, replica_groups=mesh['row'=4,'col'=8] {'row'}, dimensions={0}, use_global_device_ids=true | all-gather | bytes 163840 | tf_op jit(solution)/shard_map/all_gather | solution.py:16
  80.2 7.9 %gather_fusion = bf16[192,128,128]{2,1,0:T(8,128)(2,1)} fusion(bf16[4,128,128]{2,1,0:T(8,128)(2,1)S(1)} %bitcast.45, s32[1024]{0:T(1024)S(1)} %pad_clamp_fusion.1), kind=kCustom, calls=%fused_computation | custom fusion | bytes 12583680 | tf_op jit(solution)/shard_map/gather | solution.py:19
  88.1 11.0 %fusion.11 = f32[192,128,128]{2,1,0:T(8,128)} fusion(bf16[192,128,128]{2,1,0:T(8,128)(2,1)} %gather_fusion, bf16[1,1,192,128,128]{4,3,2,1,0:T(8,128)(2,1)} %param.11, pred[192]{0:T(512)(128)(4,1)S(1)} %iota_compare_fusion), kind=kOutput, calls=%fused_computation.40 | convolution fusion | flops 808452096 | bytes 25166016 | tf_op jit(solution)/shard_map/kab,kbw->kaw/dot_general | solution.py:18
  99.2 25.2 %scatter_fusion = f32[8,128,128]{2,1,0:T(8,128)S(1)} fusion(f32[8,128,128]{2,1,0:T(8,128)S(1)} %broadcast.292.clone, s32[192]{0:T(256)S(1)} %bitcast.49, f32[192,128,128]{2,1,0:T(8,128)} %fusion.11), kind=kCustom, calls=%fused_computation.4 | custom fusion | flops 3145728 | bytes 37749504 | tf_op jit(solution)/shard_map/scatter-add | solution.py:24
  124.5 0.8 copy-done.4
  125.3 0.0 reduce-scatter.11.cloned.1.call-start
  125.3 31.3 %reduce-scatter.5.cloned.1.call-done = f32[128,128]{1,0:T(8,128)} async-done(((f32[1024,128]{1,0:T(8,128)}), f32[128,128]{1,0:T(8,128)}) %reduce-scatter.5.cloned.1.call-update) | async-done | bytes 65552 | tf_op jit(solution)/shard_map/reduce_scatter | solution.py:26
  156.7 1.5 convert_reduce_fusion
  158.2 8.4 %all_gather.14 = bf16[512,128]{1,0:T(8,128)(2,1)S(1)} all-gather(bf16[128,128]{1,0:T(8,128)(2,1)S(1)} %get-tuple-element.10), channel_id=1, replica_groups=mesh['row'=4,'col'=8] {'row'}, dimensions={0}, use_global_device_ids=true | all-gather | bytes 163840 | tf_op jit(solution)/shard_map/all_gather | solution.py:16
  166.7 14.4 %all_gather.15 = bf16[1024,128]{1,0:T(8,128)(2,1)S(1)} all-gather(bf16[128,128]{1,0:T(8,128)(2,1)S(1)} %get-tuple-element.10), channel_id=1, replica_groups=mesh['row'=4,'col'=8] {'col'}, dimensions={0}, use_global_device_ids=true | all-gather | bytes 294912 | tf_op jit(solution)/shard_map/all_gather | solution.py:17
  181.1 7.9 %gather_fusion.2 = bf16[192,128,128]{2,1,0:T(8,128)(2,1)} fusion(bf16[4,128,128]{2,1,0:T(8,128)(2,1)S(1)} %bitcast.46, s32[1024]{0:T(1024)S(1)} %pad_clamp_fusion.1), kind=kCustom, calls=%fused_computation.2 | custom fusion | bytes 12583680 | tf_op jit(solution)/shard_map/gather | solution.py:19
  189.0 7.8 %gather_fusion.3 = bf16[192,128,128]{2,1,0:T(8,128)(2,1)} fusion(bf16[8,128,128]{2,1,0:T(8,128)(2,1)S(1)} %bitcast.47, s32[1024]{0:T(1024)S(1)} %pad_clamp_fusion), kind=kCustom, calls=%fused_computation.3 | custom fusion | bytes 12583680 | tf_op jit(solution)/shard_map/gather | solution.py:22
  196.8 11.6 %fusion.8 = f32[192,128,128]{2,1,0:T(8,128)} fusion(bf16[192,128,128]{2,1,0:T(8,128)(2,1)} %gather_fusion.3, bf16[1,1,192,128,128]{4,3,2,1,0:T(8,128)(2,1)} %param.11, pred[192]{0:T(512)(128)(4,1)S(1)} %iota_compare_fusion), kind=kOutput, calls=%fused_computation.37 | convolution fusion | flops 808452096 | bytes 25166016 | tf_op jit(solution)/shard_map/kba,kbw->kaw/dot_general | solution.py:21
  208.4 25.2 %scatter_fusion.3 = f32[4,128,128]{2,1,0:T(8,128)S(1)} fusion(f32[4,128,128]{2,1,0:T(8,128)S(1)} %broadcast.294, s32[192]{0:T(256)S(1)} %bitcast.52, f32[192,128,128]{2,1,0:T(8,128)} %fusion.8), kind=kCustom, calls=%fused_computation.7 | custom fusion | flops 3145728 | bytes 37749504 | tf_op jit(solution)/shard_map/scatter-add | solution.py:25
  233.7 0.7 copy-done.1
  234.4 11.1 %fusion.9 = f32[192,128,128]{2,1,0:T(8,128)} fusion(bf16[192,128,128]{2,1,0:T(8,128)(2,1)} %gather_fusion.2, bf16[1,1,192,128,128]{4,3,2,1,0:T(8,128)(2,1)} %param.11, pred[192]{0:T(512)(128)(4,1)S(1)} %iota_compare_fusion), kind=kOutput, calls=%fused_computation.38 | convolution fusion | flops 808452096 | bytes 25166016 | tf_op jit(solution)/shard_map/kab,kbw->kaw/dot_general | solution.py:18
  245.5 25.2 %scatter_fusion.2 = f32[8,128,128]{2,1,0:T(8,128)S(1)} fusion(f32[8,128,128]{2,1,0:T(8,128)S(1)} %broadcast.292, s32[192]{0:T(256)S(1)} %bitcast.50, f32[192,128,128]{2,1,0:T(8,128)} %fusion.9), kind=kCustom, calls=%fused_computation.6 | custom fusion | flops 3145728 | bytes 37749504 | tf_op jit(solution)/shard_map/scatter-add | solution.py:24
  270.8 0.8 copy-done.3
  271.7 28.5 %reduce-scatter.9.cloned.1.call-done = f32[128,128]{1,0:T(8,128)} async-done(((f32[1024,128]{1,0:T(8,128)}), f32[128,128]{1,0:T(8,128)}) %reduce-scatter.9.cloned.1.call-update) | async-done | bytes 65552 | tf_op jit(solution)/shard_map/reduce_scatter | solution.py:26
  300.2 1.8 convolution_bitcast_fusion
  302.0 37.9 %psum.15 = f32[128]{0:T(128)} all-reduce(f32[128]{0:T(128)S(1)} %get-tuple-element.9), channel_id=1, replica_groups=mesh['row'=4,'col'=8] {'row','col'}, use_global_device_ids=true, to_apply=%region_10.11 | all-reduce | flops 128 | bytes 1024 | tf_op jit(solution)/shard_map/psum | solution.py:52
  339.9 82.2 %all-reduce.2.cloned.1.call-done = f32[128,128]{0,1:T(8,128)} async-done(((f32[128,128]{0,1:T(8,128)}), f32[128,128]{0,1:T(8,128)}) %all-reduce.2.cloned.1.call-update) | async-done | bytes 65552 | tf_op jit(solution)/shard_map/psum | solution.py:52
  422.1 1.6 copy.16
  (27 shorter events, 0.4 us)
Async XLA Ops:
  7.2 2.1 copy-start
  7.2 118.2 %reduce-scatter.7.cloned.1.call-start = ((), (), s32[]{:S(2)}) async-start(), calls=%async_computation.5 | async-start | bytes 327680 | tf_op jit(solution)/shard_map/reduce_scatter | solution.py:27
  70.7 0.7 copy-start.2
  71.5 85.2 %reduce-scatter.5.cloned.1.call-start = ((), (), s32[]{:S(2)}) async-start(), calls=%async_computation.4 | async-start | bytes 589824 | tf_op jit(solution)/shard_map/reduce_scatter | solution.py:26
  99.2 57.5 %copy-start.5 = (bf16[128,128]{1,0:T(8,128)(2,1)S(1)}, bf16[128,128]{1,0:T(8,128)(2,1)}, u32[]{:S(2)}) copy-start(bf16[128,128]{1,0:T(8,128)(2,1)} %param.15) | copy-start | bytes 98308
  99.2 57.5 %copy-start.6 = (f32[128]{0:T(128)S(1)}, f32[128]{0:T(128)}, u32[]{:S(2)}) copy-start(f32[128]{0:T(128)} %param.10) | copy-start | bytes 1540
  124.5 0.8 copy-start.4
  125.3 146.4 %reduce-scatter.11.cloned.1.call-start = ((), (), s32[]{:S(2)}) async-start(), calls=%async_computation.7 | async-start | bytes 327680 | tf_op jit(solution)/shard_map/reduce_scatter | solution.py:27
  233.6 0.7 copy-start.1
  234.4 65.8 %reduce-scatter.9.cloned.1.call-start = ((), (), s32[]{:S(2)}) async-start(), calls=%async_computation.6 | async-start | bytes 589824 | tf_op jit(solution)/shard_map/reduce_scatter | solution.py:26
  270.8 0.8 copy-start.3
  271.6 150.5 %all-reduce.2.cloned.1.call-start = ((), (), s32[]{:S(2)}) async-start(), calls=%async_computation.8 | async-start | bytes 131072 | tf_op jit(solution)/shard_map/psum | solution.py:52
Sparse Core Ops, SparseCore 0:
  71.6 25.3 reduce-scatter.6
  125.4 31.2 reduce-scatter.4
  234.5 21.5 reduce-scatter.10
  271.7 28.4 reduce-scatter.8
  306.2 115.8 all-reduce.1
where the time goes:
time: 434 us; the launch traced here: 430 us
  waiting for transfers between devices  142 us (33%)
  other arithmetic  104 us (24%)
  blocking collectives  85.2 us (20%)
  matrix products  48 us (11%)
  local copies, waits for them, and re-layouts  36.1 us (8%)
  between operations  14.6 us (3%)
    psum x1, waiting for transfers between devices, on_device(): lax.psum((local_weight, local_bias), ('row', 'col'))  82.2 us
    reduce_scatter x2, waiting for transfers between devices, aggregate(): lax.psum_scatter(row_sums.reshape(-1, width), 'col', scatter_dimension=0,...  59.9 us
    scatter-add x2, other arithmetic, aggregate(): jax.ops.segment_sum(mirror_terms, col_slot, num_segments=group_cols)  50.5 us
    scatter-add x2, other arithmetic, aggregate(): jax.ops.segment_sum(forward_terms, row_slot, num_segments=group_rows)  50.5 us
    psum x1, blocking collectives, on_device(): lax.psum((local_weight, local_bias), ('row', 'col'))  37.9 us
    all_gather x2, blocking collectives, aggregate(): lax.all_gather(feats, 'col', axis=0, tiled=True).reshape(-1, block, width)  30.3 us
    dot_general x2, matrix products, aggregate(): jnp.einsum('kba,kbw->kaw', matrices, row_side[row_slot], preferred_elemen...  23.2 us
    dot_general x2, matrix products, aggregate(): jnp.einsum('kab,kbw->kaw', matrices, col_side[col_slot], preferred_elemen...  22.1 us
  transfers between devices with their start and end apart: 5, of which 3 were waited for; matrix products, arithmetic and copies ran while one was open for 19% of the time, Pallas kernels for 0%

commit v1 on v0

v1 whole, which is shorter than its diff:
```python
import functools

import jax
import jax.numpy as jnp
from jax import lax
from jax.experimental import pallas as pl
from jax.experimental.pallas import tpu as pltpu
from jax.sharding import PartitionSpec as P

F32 = jnp.float32
BF16 = jnp.bfloat16
MESH = pl.DeviceIdType.MESH
MIB = 1024 * 1024


def gelu_parts(pre):
    cdf = 0.5 * (1.0 + lax.erf(pre * 0.7071067811865476))
    dens = jnp.exp(-0.5 * pre * pre) * 0.3989422804014327
    return (pre * cdf, cdf + pre * dens)


def densify(n_row, n_col, chunk, rows_ref, cols_ref, count_ref, values_ref, tiles_ref, held, even, odd, sems):
    block = values_ref.shape[-1]
    tiles = n_row * n_col
    half = n_col // 2
    count = count_ref[0, 0]
    chunks = lax.div(count + chunk - 1, chunk)

    def fetch(i):
        part = pl.ds(i * chunk, chunk)
        return pltpu.make_async_copy(values_ref.at[0, 0, part], held.at[part], sems.at[i])

    @pl.loop(0, chunks)
    def _(i):
        fetch(i).start()

    @pl.loop(0, tiles)
    def _(t):
        even[t] = jnp.zeros((block, block), F32)
        odd[t] = jnp.zeros((block, block), F32)

    @pl.loop(0, chunks)
    def _(i):
        fetch(i).wait()
        for s in range(0, chunk, 2):
            for step, acc in ((0, even), (1, odd)):
                k = i * chunk + s + step
                row = lax.div(rows_ref[0, 0, k], n_row)
                place = lax.rem(row, 2) * half + lax.div(row, 2)
                tile = place * n_row + lax.rem(cols_ref[0, 0, k], n_row)
                tile = jnp.where(k < count, tile, tiles)
                acc[tile] = acc[tile] + held[k].astype(F32)

    for p in range(n_col):
        for q in range(n_row):
            t = p * n_row + q
            tiles_ref[p * block:(p + 1) * block, q * block:(q + 1) * block] = (even[t] + odd[t]).astype(BF16)


def layer(
    n_row, n_col, tiles_ref, x_ref, w_ref, bias_ref, cot_ref, act_ref, wg_ref, bg_ref,
    xcol, xrow, half_out, half_in, sum_out, sum_in, mir_out, mir_in, part, red1, red2, red3,
    s_xrow, r_xrow, s_xz, r_xz, s_xp, r_xp, s_half, r_half, s_sum, r_sum, s_mir, r_mir,
    s_1, r_1, s_2, r_2, s_3, r_3,
):
    r = lax.axis_index("row")
    c = lax.axis_index("col")
    block = x_ref.shape[0]
    n_z = n_col // 2
    z = lax.div(c, 2)
    core = lax.rem(c, 2)
    mate = 1 - core
    mate_id = (r, z * 2 + mate)
    here = core * n_z + z
    n_part, part_rows = part.shape[0], part.shape[1] - 8
    sends = []

    def rows_of(index):
        return pl.ds(pl.multiple_of(index * block, block), block)

    def copy(src, dst, send, recv, device):
        return pltpu.make_async_remote_copy(
            src_ref=src, dst_ref=dst, send_sem=send, recv_sem=recv, device_id=device, device_id_type=MESH
        )

    def send(src, dst, s, t, device):
        one = copy(src, dst, s, t, device)
        one.start()
        sends.append(one)

    def row_at(d):
        return lax.rem(r + d, n_row)

    def z_at(d):
        return lax.rem(z + d, n_z)

    def col_at(d):
        return lax.rem(c + d, n_col)

    barrier = pltpu.get_barrier_semaphore()
    for d in range(1, n_row):
        pl.semaphore_signal(barrier, inc=1, device_id=(row_at(d), c), device_id_type=MESH)
    for d in range(1, n_col):
        pl.semaphore_signal(barrier, inc=1, device_id=(r, col_at(d)), device_id_type=MESH)
    x = x_ref[...]
    xcol[rows_of(r), :] = x
    xrow[here] = x.T
    pl.semaphore_wait(barrier, n_row + n_col - 2)

    for d in range(1, n_row):
        send(xcol.at[rows_of(r)], xcol.at[rows_of(r)], s_xrow.at[d - 1], r_xrow.at[d - 1], (row_at(d), c))
    for d in range(1, n_z):
        send(xrow.at[here], xrow.at[here], s_xz.at[d - 1], r_xz.at[d - 1], (r, z_at(d) * 2 + core))
    send(xrow.at[here], xrow.at[here], s_xp.at[0], r_xp.at[0], mate_id)

    for d in range(1, n_row):
        slot = xcol.at[rows_of(row_at(n_row - d))]
        copy(slot, slot, s_xrow.at[d - 1], r_xrow.at[d - 1], (row_at(d), c)).wait_recv()

    span = n_z * block
    there = tiles_ref[pl.ds(pl.multiple_of(mate * span, span), span), :]
    xc = xcol[...]
    half_out[...] = jnp.dot(there, xc, preferred_element_type=F32).astype(BF16)
    send(half_out, half_in, s_half.at[0], r_half.at[0], mate_id)
    mine = tiles_ref[pl.ds(pl.multiple_of(core * span, span), span), :]
    own = jnp.dot(mine, xc, preferred_element_type=F32)

    for d in range(1, n_z):
        slot = xrow.at[core * n_z + z_at(n_z - d)]
        copy(slot, slot, s_xz.at[d - 1], r_xz.at[d - 1], mate_id).wait_recv()
        send(slot, slot, s_xp.at[d], r_xp.at[d], mate_id)

    copy(half_out, half_in, s_half.at[0], r_half.at[0], mate_id).wait_recv()
    total = (own + half_in[...].astype(F32)).astype(BF16)
    sum_out[...] = total
    for d in range(1, n_z):
        send(
            sum_out.at[rows_of(z_at(d))], sum_in.at[d - 1], s_sum.at[d - 1], r_sum.at[d - 1],
            (r, z_at(d) * 2 + core),
        )

    for d in range(n_z):
        slot = xrow.at[mate * n_z + z_at(n_z - d)]
        copy(slot, slot, s_xp.at[d], r_xp.at[d], mate_id).wait_recv()

    xt = jnp.concatenate([xrow[i] for i in range(n_col)], axis=1)
    for q in range(n_row // 2):
        both = jnp.dot(xt, tiles_ref[:, 2 * q * block:2 * (q + 1) * block], preferred_element_type=F32).astype(BF16)
        mir_out[2 * q] = both[:, :block]
        mir_out[2 * q + 1] = both[:, block:]
    for d in range(1, n_row):
        send(mir_out.at[row_at(d)], mir_in.at[d - 1], s_mir.at[d - 1], r_mir.at[d - 1], (row_at(d), c))

    y = sum_out[rows_of(z), :].astype(F32)
    for d in range(1, n_z):
        copy(sum_in.at[d - 1], sum_in.at[d - 1], s_sum.at[d - 1], r_sum.at[d - 1], mate_id).wait_recv()
        y = y + sum_in[d - 1].astype(F32)
    yt = mir_out[r].astype(F32)
    for d in range(1, n_row):
        copy(mir_in.at[d - 1], mir_in.at[d - 1], s_mir.at[d - 1], r_mir.at[d - 1], mate_id).wait_recv()
        yt = yt + mir_in[d - 1].astype(F32)
    y = y + yt.T

    high = y.astype(BF16)
    low = (y - high.astype(F32)).astype(BF16)
    w = w_ref[...]
    pre = (
        jnp.dot(high, w, preferred_element_type=F32)
        + jnp.dot(low, w, preferred_element_type=F32)
        + bias_ref[...].reshape(1, -1)
    )
    act, slope = gelu_parts(pre)
    act_ref[...] = act.astype(BF16)
    grad = (cot_ref[...].astype(F32) * slope).astype(BF16)
    local = jnp.dot(high.T, grad, preferred_element_type=F32) + jnp.dot(low.T, grad, preferred_element_type=F32)
    local_bias = jnp.broadcast_to(jnp.sum(grad.astype(F32), axis=0, keepdims=True), (8, grad.shape[1]))
    for j in range(n_part):
        part[j, :part_rows, :] = local[j * part_rows:(j + 1) * part_rows, :]
        part[j, part_rows:, :] = local_bias

    red1[c] = part[lax.rem(c, n_part)]
    for d in range(1, n_col):
        to = col_at(d)
        send(part.at[lax.rem(to, n_part)], red1.at[c], s_1.at[d - 1], r_1.at[d - 1], (r, to))
    for d in range(1, n_col):
        slot = red1.at[col_at(n_col - d)]
        copy(slot, slot, s_1.at[d - 1], r_1.at[d - 1], mate_id).wait_recv()
    red2[r] = functools.reduce(lambda a, b: a + b, [red1[i] for i in range(n_col)])
    for d in range(1, n_row):
        send(red2.at[r], red2.at[r], s_2.at[d - 1], r_2.at[d - 1], (row_at(d), c))
    for d in range(1, n_row):
        slot = red2.at[row_at(n_row - d)]
        copy(slot, slot, s_2.at[d - 1], r_2.at[d - 1], mate_id).wait_recv()
    done = functools.reduce(lambda a, b: a + b, [red2[i] for i in range(n_row)])
    bg_ref[...] = done[part_rows:part_rows + 1, :]
    red3[c] = done[:part_rows, :]
    for d in range(1, n_col):
        send(red3.at[c], red3.at[c], s_3.at[d - 1], r_3.at[d - 1], (r, col_at(d)))
    for d in range(1, n_col):
        slot = red3.at[col_at(n_col - d)]
        copy(slot, slot, s_3.at[d - 1], r_3.at[d - 1], mate_id).wait_recv()
    for j in range(n_part):
        wg_ref[j * part_rows:(j + 1) * part_rows, :] = red3[j]
    for one in sends:
        one.wait_send()


def on_device(n_row, n_col, x_feats, weight, bias, block_values, block_rows, block_cols, block_counts, cotangent):
    slots, block = block_values.shape[2], block_values.shape[-1]
    nodes, f_in = x_feats.shape
    f_out = weight.shape[1]
    assert nodes == block and n_col % 2 == 0 and n_row % 2 == 0
    tiles = n_row * n_col
    chunk = 16 if slots % 16 == 0 else slots
    vmem = pl.BlockSpec(memory_space=pltpu.VMEM)
    smem = pl.BlockSpec(memory_space=pltpu.SMEM)
    dense_bytes = slots * block * block * 2 + (2 * (tiles + 1) * 4 + tiles * 2) * block * block
    dense = pl.pallas_call(
        functools.partial(densify, n_row, n_col, chunk),
        out_shape=jax.ShapeDtypeStruct((n_col * block, n_row * block), BF16),
        in_specs=[smem, smem, smem, pl.BlockSpec(memory_space=pl.ANY)],
        out_specs=vmem,
        scratch_shapes=[
            pltpu.VMEM((slots, block, block), BF16),
            pltpu.VMEM((tiles + 1, block, block), F32),
            pltpu.VMEM((tiles + 1, block, block), F32),
            pltpu.SemaphoreType.DMA((slots // chunk,)),
        ],
        compiler_params=pltpu.CompilerParams(vmem_limit_bytes=dense_bytes + 4 * MIB),
        cost_estimate=pl.CostEstimate(flops=slots * block * block, bytes_accessed=slots * block * block * 2, transcendentals=0),
        name="densify",
    )(block_rows, block_cols, block_counts, block_values)

    n_z = n_col // 2
    n_part = min(n_col, f_in // 8)
    part_rows = f_in // n_part
    pairs = []
    for count in (n_row - 1, n_z - 1, n_z, 1, n_z - 1, n_row - 1, n_col - 1, n_row - 1, n_col - 1):
        pairs += [pltpu.SemaphoreType.DMA((count,))] * 2
    act, weight_grad, bias_grad = pl.pallas_call(
        functools.partial(layer, n_row, n_col),
        out_shape=(
            jax.ShapeDtypeStruct((nodes, f_out), BF16),
            jax.ShapeDtypeStruct((f_in, f_out), F32),
            jax.ShapeDtypeStruct((1, f_out), F32),
        ),
        in_specs=[vmem] * 5,
        out_specs=(vmem, vmem, vmem),
        scratch_shapes=[
            pltpu.VMEM((n_row * block, f_in), BF16),
            pltpu.VMEM((n_col, f_in, block), BF16),
            pltpu.VMEM((n_z * block, f_in), BF16),
            pltpu.VMEM((n_z * block, f_in), BF16),
            pltpu.VMEM((n_z * block, f_in), BF16),
            pltpu.VMEM((n_z - 1, block, f_in), BF16),
            pltpu.VMEM((n_row, f_in, block), BF16),
            pltpu.VMEM((n_row - 1, f_in, block), BF16),
            pltpu.VMEM((n_part, part_rows + 8, f_out), F32),
            pltpu.VMEM((n_col, part_rows + 8, f_out), F32),
            pltpu.VMEM((n_row, part_rows + 8, f_out), F32),
            pltpu.VMEM((n_col, part_rows, f_out), F32),
            *pairs,
        ],
        compiler_params=pltpu.CompilerParams(
            collective_id=0, has_side_effects=True, vmem_limit_bytes=tiles * block * block * 2 + 16 * MIB
        ),
        cost_estimate=pl.CostEstimate(
            flops=4 * tiles * block * block * f_in, bytes_accessed=tiles * block * block * 2, transcendentals=0
        ),
        name="layer",
    )(dense, x_feats, weight, bias, cotangent)
    return act, weight_grad, bias_grad.reshape(f_out)


def solution(mesh):
    in_specs = (
        P(("col", "row"), None),
        P(),
        P(),
        P("row", "col", None, None, None),
        P("row", "col", None),
        P("row", "col", None),
        P("row", "col"),
        P(("col", "row"), None),
    )
    out_specs = (P(("col", "row"), None), P(), P())
    return jax.shard_map(
        functools.partial(on_device, mesh.shape["row"], mesh.shape["col"]),
        mesh=mesh, in_specs=in_specs, out_specs=out_specs, check_vma=False,
    )
```

time: 434 us -> 38.3 us (0.09)
  waiting for transfers between devices: 142 us -> 0 us
  other arithmetic: 104 us -> 0 us
  blocking collectives: 85.2 us -> 0 us
  matrix products: 48 us -> 0 us
  Pallas kernels: 0 us -> 30.8 us
  local copies, waits for them, and re-layouts: 36.1 us -> 5.91 us
  between operations: 14.6 us -> 1.36 us
    scatter-add x4 -> x0, other arithmetic: 101 us -> none  [the longest x2 50.5 us: aggregate(): jax.ops.segment_sum(mirror_terms, col_slot, num_segments=group_cols)]
    psum x1 -> x0, waiting for transfers between devices: 82.2 us -> none  [on_device(): lax.psum((local_weight, local_bias), ('row', 'col'))]
    reduce_scatter x4 -> x0, waiting for transfers between devices: 59.9 us -> none  [the longest x2 59.9 us: aggregate(): lax.psum_scatter(row_sums.reshape(-1, width), 'col', scatter_dimension=0,...]
    dot_general x6 -> x0, matrix products: 48 us -> none  [the longest x2 23.2 us: aggregate(): jnp.einsum('kba,kbw->kaw', matrices, row_side[row_slot], preferred_elemen...]
    all_gather x4 -> x0, blocking collectives: 47.4 us -> none  [the longest x2 30.3 us: aggregate(): lax.all_gather(feats, 'col', axis=0, tiled=True).reshape(-1, block, width)]
    psum x1 -> x0, blocking collectives: 37.9 us -> none  [on_device(): lax.psum((local_weight, local_bias), ('row', 'col'))]
    gather x4 -> x0, local copies, waits for them, and re-layouts: 31.4 us -> none  [the longest x2 15.8 us: aggregate(): col_side[col_slot]]
    pallas_call x0 -> x2, Pallas kernels: none -> 30.8 us  [the longest x1 29.3 us: on_device(): pl.pallas_call(functools.partial(layer, n_row, n_col), out_shape=(jax.Sha...]
  transfers between devices with their start and end apart: 5 -> 0, of which waited for: 3 -> 0; matrix products, arithmetic and copies ran while one was open for 19% -> 0% of each run, Pallas kernels for 0% -> 0%
where the time goes in v1:
time: 38.3 us; the launch traced here: 38.1 us
  Pallas kernels  30.8 us (80%)
  local copies, waits for them, and re-layouts  5.91 us (15%)
  between operations  1.36 us (4%)
    pallas_call x1, Pallas kernels, on_device(): pl.pallas_call(functools.partial(layer, n_row, n_col), out_shape=(jax.Sha...  29.3 us
    unnamed x17, local copies, waits for them, and re-layouts  5.91 us
    pallas_call x1, Pallas kernels, on_device(): pl.pallas_call(functools.partial(densify, n_row, n_col, chunk), out_shape...  1.55 us

profile of v1, /device:TPU:0, one launch (start us, length us, event | category | flops | bytes accessed | tf_op | source)
XLA Modules:
  0.0 38.1 jit_solution(15168245417536463323)
XLA Ops:
  0.6 0.0 copy-start.6
  1.3 0.0 copy-start
  1.3 2.8 %copy-done = bf16[1,1,192,128,128]{4,3,2,1,0:T(8,128)(2,1)S(1)} copy-done((bf16[1,1,192,128,128]{4,3,2,1,0:T(8,128)(2,1)S(1)}, bf16[1,1,192,128,128]{4,3,2,1,0:T(8,128)(2,1)}, u32[]{:S(2)}) %copy-start) | copy-done | bytes 6291480
  4.1 0.0 copy-start.4
  4.1 0.7 %copy-done.4 = s32[1,1,192]{2,1,0:T(1,128)S(1)} copy-done((s32[1,1,192]{2,1,0:T(1,128)S(1)}, s32[1,1,192]{2,1,0:T(1,128)}, u32[]{:S(2)}) %copy-start.4) | copy-done | bytes 792
  4.8 0.0 copy-start.5
  4.8 0.7 %copy-done.5 = s32[1,1,192]{2,1,0:T(1,128)S(1)} copy-done((s32[1,1,192]{2,1,0:T(1,128)S(1)}, s32[1,1,192]{2,1,0:T(1,128)}, u32[]{:S(2)}) %copy-start.5) | copy-done | bytes 792
  5.4 0.0 copy-start.1
  5.4 0.0 copy-start.2
  5.5 0.0 copy-start.3
  5.5 1.6 %densify.1.tiles_ref = bf16[1024,512]{1,0:T(8,128)(2,1)S(1)} custom-call(s32[1,1,192]{2,1,0:T(1,128)S(1)} %copy-done.4, s32[1,1,192]{2,1,0:T(1,128)S(1)} %copy-done.5, s32[1,1]{1,0:T(1,128)S(6)} %copy.14.count_ref, bf16[1,1,192,128,128]{4,3,2,1,0:T(8,128)(2,1)S(1)} %copy-done), custom_call_target="tpu_custom_call" | custom-call | flops 3145728 | bytes 6291456 | tf_op jit(solution)/shard_map/densify/pallas_call | solution.py:218
  7.0 0.0 copy-done.6
  7.0 0.0 copy-done.1
  7.0 0.0 copy-done.2
  7.0 0.0 copy-done.3
  7.1 29.3 %layer.1 = (bf16[128,128]{1,0:T(8,128)(2,1)S(1)}, f32[128,128]{1,0:T(8,128)S(1)}, f32[1,128]{1,0:T(1,128)S(1)}) custom-call(bf16[1024,512]{1,0:T(8,128)(2,1)S(1)} %densify.1.tiles_ref, bf16[128,128]{1,0:T(8,128)(2,1)S(1)} %copy-done.1, bf16[128,128]{1,0:T(8,128)(2,1)S(1)} %copy-done.2, f32[128]{0:T(128)S(1)} %copy-done.6, bf16[128,128]{1,0:T(8,128)(2,1)S(1)} %copy-done.3), custom_call_target="tpu_custom_call" | custom-call | flops 268435456 | bytes 1048576 | tf_op jit(solution)/shard_map/layer/pallas_call | solution.py:240
  36.3 0.6 %copy.15 = bf16[128,128]{1,0:T(8,128)(2,1)} copy(bf16[128,128]{1,0:T(8,128)(2,1)S(1)} %get-tuple-element.12) | data formatting | bytes 65536
  37.0 0.6 %copy.16 = f32[128,128]{1,0:T(8,128)} copy(f32[128,128]{1,0:T(8,128)S(1)} %get-tuple-element.13) | data formatting | bytes 131072
  37.6 0.5 %copy.17 = f32[128]{0:T(128)} copy(f32[128]{0:T(128)S(1)} %bitcast.1) | data formatting | bytes 1024
Async XLA Ops:
  0.6 6.4 %copy-start.6 = (f32[128]{0:T(128)S(1)}, f32[128]{0:T(128)}, u32[]{:S(2)}) copy-start(f32[128]{0:T(128)} %bias_ref.1) | copy-start | bytes 1540
  1.3 2.8 %copy-start = (bf16[1,1,192,128,128]{4,3,2,1,0:T(8,128)(2,1)S(1)}, bf16[1,1,192,128,128]{4,3,2,1,0:T(8,128)(2,1)}, u32[]{:S(2)}) copy-start(bf16[1,1,192,128,128]{4,3,2,1,0:T(8,128)(2,1)} %values_ref.1) | copy-start | bytes 18874372
  4.1 0.7 %copy-start.4 = (s32[1,1,192]{2,1,0:T(1,128)S(1)}, s32[1,1,192]{2,1,0:T(1,128)}, u32[]{:S(2)}) copy-start(s32[1,1,192]{2,1,0:T(1,128)} %rows_ref.1) | copy-start | bytes 2308
  4.8 0.7 %copy-start.5 = (s32[1,1,192]{2,1,0:T(1,128)S(1)}, s32[1,1,192]{2,1,0:T(1,128)}, u32[]{:S(2)}) copy-start(s32[1,1,192]{2,1,0:T(1,128)} %cols_ref.1) | copy-start | bytes 2308
  5.4 1.6 %copy-start.1 = (bf16[128,128]{1,0:T(8,128)(2,1)S(1)}, bf16[128,128]{1,0:T(8,128)(2,1)}, u32[]{:S(2)}) copy-start(bf16[128,128]{1,0:T(8,128)(2,1)} %x_ref.1) | copy-start | bytes 98308
  5.4 1.6 %copy-start.2 = (bf16[128,128]{1,0:T(8,128)(2,1)S(1)}, bf16[128,128]{1,0:T(8,128)(2,1)}, u32[]{:S(2)}) copy-start(bf16[128,128]{1,0:T(8,128)(2,1)} %w_ref.1) | copy-start | bytes 98308
  5.5 1.6 %copy-start.3 = (bf16[128,128]{1,0:T(8,128)(2,1)S(1)}, bf16[128,128]{1,0:T(8,128)(2,1)}, u32[]{:S(2)}) copy-start(bf16[128,128]{1,0:T(8,128)(2,1)} %cot_ref.1) | copy-start | bytes 98308

commit v2 on v1

v2 whole, which is shorter than its diff:
```python
import functools

import jax
import jax.numpy as jnp
from jax import lax
from jax.experimental import pallas as pl
from jax.experimental.pallas import tpu as pltpu
from jax.sharding import PartitionSpec as P

F32 = jnp.float32
BF16 = jnp.bfloat16
MESH = pl.DeviceIdType.MESH
MIB = 1024 * 1024


def gelu_parts(pre):
    cdf = 0.5 * (1.0 + lax.erf(pre * 0.7071067811865476))
    dens = jnp.exp(-0.5 * pre * pre) * 0.3989422804014327
    return (pre * cdf, cdf + pre * dens)


def sort_slots(n_row, n_col, rows_ref, cols_ref, count_ref, keys, order):
    slots = rows_ref.shape[-1]
    log_row = n_row.bit_length() - 1
    row = jnp.right_shift(rows_ref[0], log_row)
    place = jnp.bitwise_and(row, 1) * (n_col // 2) + jnp.right_shift(row, 1)
    tile = place * n_row + jnp.bitwise_and(cols_ref[0], n_row - 1)
    index = lax.broadcasted_iota(jnp.int32, (1, slots), 1)
    tile = jnp.where(index < count_ref[...], tile, n_row * n_col)
    keys[...] = n_row * n_col * 256 + lax.broadcasted_iota(jnp.int32, keys.shape, 1)
    keys[0:1, 0:slots] = tile * 256 + index
    along = jnp.broadcast_to(keys[0:1, :], (256, 256))
    down = along.T
    rank = jnp.sum((along < down).astype(jnp.int32), axis=1, keepdims=True)
    lane = lax.broadcasted_iota(jnp.int32, (256, 256), 1)
    order[0:1, :] = jnp.sum(jnp.where(rank == lane, down, 0), axis=0, keepdims=True)
    order[1:2, :] = jnp.sum((jnp.right_shift(down, 8) <= lane).astype(jnp.int32), axis=0, keepdims=True)
    order[2:, :] = jnp.zeros((order.shape[0] - 2, 256), jnp.int32)


def build_tiles(n_row, n_col, order, held, runs, tiles_ref):
    slots, block = held.shape[0], held.shape[1]

    def step(i, carry):
        total, before = carry
        key = order[0, i]
        tile = jnp.right_shift(key, 8)
        slot = jnp.minimum(jnp.bitwise_and(key, 255), slots - 1)
        total = jnp.where(tile == before, total, 0.0) + held[slot].astype(F32)
        runs[i] = total.astype(BF16)
        return total, tile

    lax.fori_loop(0, slots, step, (jnp.zeros((block, block), F32), jnp.int32(-1)), unroll=4)

    def place(p, before):
        for q in range(n_row):
            end = order[1, p * n_row + q]
            value = runs[jnp.maximum(end - 1, 0)]
            rows = pl.ds(pl.multiple_of(p * block, block), block)
            tiles_ref[rows, q * block:(q + 1) * block] = jnp.where(end > before, value, jnp.zeros_like(value))
            before = end
        return before

    lax.fori_loop(0, n_col, place, jnp.int32(0))


def layer(
    n_row, n_col, rows_ref, cols_ref, count_ref, values_ref, x_ref, w_ref, bias_ref, cot_ref,
    act_ref, wg_ref, bg_ref,
    held, runs, tiles_ref, keys, order, order_smem, values_sem, order_sem,
    xcol, xrow, half_out, half_in, sum_out, sum_in, mir_out, mir_in, pair_out, pair_in, over_z, over_row, final,
    s_xrow, r_xrow, s_xz, r_xz, s_xp, r_xp, s_half, r_half, s_sum, r_sum, s_mir, r_mir,
    s_1, r_1, s_2, r_2, s_3, r_3, s_4, r_4,
):
    fetch = pltpu.make_async_copy(values_ref.at[0, 0], held, values_sem)
    fetch.start()
    r = lax.axis_index("row")
    c = lax.axis_index("col")
    block = x_ref.shape[0]
    n_z = n_col // 2
    z = lax.div(c, 2)
    core = lax.rem(c, 2)
    mate = 1 - core
    mate_id = (r, z * 2 + mate)
    here = core * n_z + z
    sends = []

    def rows_of(index):
        return pl.ds(pl.multiple_of(index * block, block), block)

    def copy(src, dst, send, recv, device):
        return pltpu.make_async_remote_copy(
            src_ref=src, dst_ref=dst, send_sem=send, recv_sem=recv, device_id=device, device_id_type=MESH
        )

    def send(src, dst, s, t, device):
        one = copy(src, dst, s, t, device)
        one.start()
        sends.append(one)

    def row_at(d):
        return lax.rem(r + d, n_row)

    def z_at(d):
        return lax.rem(z + d, n_z)

    barrier = pltpu.get_barrier_semaphore()
    for d in range(1, n_row):
        pl.semaphore_signal(barrier, inc=1, device_id=(row_at(d), c), device_id_type=MESH)
    for d in range(1, n_z):
        pl.semaphore_signal(barrier, inc=1, device_id=(r, z_at(d) * 2 + core), device_id_type=MESH)
    pl.semaphore_signal(barrier, inc=1, device_id=mate_id, device_id_type=MESH)
    x = x_ref[...]
    xcol[rows_of(r), :] = x
    xrow[here] = x.T
    sort_slots(n_row, n_col, rows_ref, cols_ref, count_ref, keys, order)
    to_smem = pltpu.make_async_copy(order, order_smem, order_sem)
    to_smem.start()
    pl.semaphore_wait(barrier, n_row + n_z - 1)

    for d in range(1, n_row):
        send(xcol.at[rows_of(r)], xcol.at[rows_of(r)], s_xrow.at[d - 1], r_xrow.at[d - 1], (row_at(d), c))
    for d in range(1, n_z):
        send(xrow.at[here], xrow.at[here], s_xz.at[d - 1], r_xz.at[d - 1], (r, z_at(d) * 2 + core))
    send(xrow.at[here], xrow.at[here], s_xp.at[0], r_xp.at[0], mate_id)

    to_smem.wait()
    fetch.wait()
    build_tiles(n_row, n_col, order_smem, held, runs, tiles_ref)

    for d in range(1, n_row):
        slot = xcol.at[rows_of(row_at(n_row - d))]
        copy(slot, slot, s_xrow.at[d - 1], r_xrow.at[d - 1], (row_at(d), c)).wait_recv()

    span = n_z * block
    there = tiles_ref[pl.ds(pl.multiple_of(mate * span, span), span), :]
    xc = xcol[...]
    half_out[...] = jnp.dot(there, xc, preferred_element_type=F32).astype(BF16)
    send(half_out, half_in, s_half.at[0], r_half.at[0], mate_id)
    mine = tiles_ref[pl.ds(pl.multiple_of(core * span, span), span), :]
    own = jnp.dot(mine, xc, preferred_element_type=F32)

    for d in range(1, n_z):
        slot = xrow.at[core * n_z + z_at(n_z - d)]
        copy(slot, slot, s_xz.at[d - 1], r_xz.at[d - 1], mate_id).wait_recv()
        send(slot, slot, s_xp.at[d], r_xp.at[d], mate_id)

    copy(half_out, half_in, s_half.at[0], r_half.at[0], mate_id).wait_recv()
    total = (own + half_in[...].astype(F32)).astype(BF16)
    sum_out[...] = total
    for d in range(1, n_z):
        send(
            sum_out.at[rows_of(z_at(d))], sum_in.at[d - 1], s_sum.at[d - 1], r_sum.at[d - 1],
            (r, z_at(d) * 2 + core),
        )

    for d in range(n_z):
        slot = xrow.at[mate * n_z + z_at(n_z - d)]
        copy(slot, slot, s_xp.at[d], r_xp.at[d], mate_id).wait_recv()

    xt = jnp.concatenate([xrow[i] for i in range(n_col)], axis=1)
    for q in range(n_row // 2):
        both = jnp.dot(xt, tiles_ref[:, 2 * q * block:2 * (q + 1) * block], preferred_element_type=F32).astype(BF16)
        mir_out[2 * q] = both[:, :block]
        mir_out[2 * q + 1] = both[:, block:]
    for d in range(1, n_row):
        send(mir_out.at[row_at(d)], mir_in.at[d - 1], s_mir.at[d - 1], r_mir.at[d - 1], (row_at(d), c))

    y = sum_out[rows_of(z), :].astype(F32)
    for d in range(1, n_z):
        copy(sum_in.at[d - 1], sum_in.at[d - 1], s_sum.at[d - 1], r_sum.at[d - 1], mate_id).wait_recv()
        y = y + sum_in[d - 1].astype(F32)
    yt = mir_out[r].astype(F32)
    for d in range(1, n_row):
        copy(mir_in.at[d - 1], mir_in.at[d - 1], s_mir.at[d - 1], r_mir.at[d - 1], mate_id).wait_recv()
        yt = yt + mir_in[d - 1].astype(F32)
    y = y + yt.T

    high = y.astype(BF16)
    low = (y - high.astype(F32)).astype(BF16)
    w = w_ref[...]
    pre = (
        jnp.dot(high, w, preferred_element_type=F32)
        + jnp.dot(low, w, preferred_element_type=F32)
        + bias_ref[...].reshape(1, -1)
    )
    act, slope = gelu_parts(pre)
    act_ref[...] = act.astype(BF16)
    grad = (cot_ref[...].astype(F32) * slope).astype(BF16)
    local = jnp.dot(high.T, grad, preferred_element_type=F32) + jnp.dot(low.T, grad, preferred_element_type=F32)
    bias_sum = jnp.sum(grad.astype(F32), axis=0, keepdims=True)

    f_out = grad.shape[1]
    h = local.shape[0] // 2
    line = lax.broadcasted_iota(jnp.int32, (16, f_out), 0)

    def packed(weight_terms, bias_terms):
        upper = bias_terms.astype(BF16).astype(F32)
        tail = jnp.where(line == 0, upper, jnp.where(line == 1, bias_terms - upper, 0.0))
        return jnp.concatenate([weight_terms, tail], axis=0).astype(BF16)

    def summed(ref):
        total = functools.reduce(lambda a, b: a + b, [ref[i].astype(F32) for i in range(ref.shape[0])])
        return total[:h, :], total[h:h + 1, :] + total[h + 1:h + 2, :]

    for j in range(2):
        pair_out[j, :h, :] = local[j * h:(j + 1) * h, :]
        pair_out[j, h:, :] = jnp.broadcast_to(bias_sum, (8, f_out))
    send(pair_out.at[mate], pair_in, s_1.at[0], r_1.at[0], mate_id)
    copy(pair_in, pair_in, s_1.at[0], r_1.at[0], mate_id).wait_recv()
    both = pair_out[core] + pair_in[...]
    over_z[z] = packed(both[:h, :], both[h:h + 1, :])
    for d in range(1, n_z):
        send(over_z.at[z], over_z.at[z], s_2.at[d - 1], r_2.at[d - 1], (r, z_at(d) * 2 + core))
    for d in range(1, n_z):
        slot = over_z.at[z_at(n_z - d)]
        copy(slot, slot, s_2.at[d - 1], r_2.at[d - 1], mate_id).wait_recv()
    over_row[r] = packed(*summed(over_z))
    for d in range(1, n_row):
        send(over_row.at[r], over_row.at[r], s_3.at[d - 1], r_3.at[d - 1], (row_at(d), c))
    for d in range(1, n_row):
        slot = over_row.at[row_at(n_row - d)]
        copy(slot, slot, s_3.at[d - 1], r_3.at[d - 1], mate_id).wait_recv()
    weight_sum, bias_total = summed(over_row)
    bg_ref[...] = bias_total
    final[core] = weight_sum
    send(final.at[core], final.at[core], s_4.at[0], r_4.at[0], mate_id)
    slot = final.at[mate]
    copy(slot, slot, s_4.at[0], r_4.at[0], mate_id).wait_recv()
    for j in range(2):
        wg_ref[j * h:(j + 1) * h, :] = final[j]
    for one in sends:
        one.wait_send()


def finish(act_ref, wg_ref, bg_ref, act_out, wg_out, bg_out, sems):
    copies = [
        pltpu.make_async_copy(src, dst, sems.at[i])
        for i, (src, dst) in enumerate(((act_ref, act_out), (wg_ref, wg_out), (bg_ref, bg_out)))
    ]
    for one in copies:
        one.start()
    for one in copies:
        one.wait()


def on_device(n_row, n_col, x_feats, weight, bias, block_values, block_rows, block_cols, block_counts, cotangent):
    slots, block = block_values.shape[2], block_values.shape[-1]
    nodes, f_in = x_feats.shape
    f_out = weight.shape[1]
    assert nodes == block and slots <= 256 and n_row * n_col <= 256
    assert n_col % 2 == 0 and n_row % 2 == 0 and n_row & (n_row - 1) == 0
    tiles = n_row * n_col
    vmem = pl.BlockSpec(memory_space=pltpu.VMEM)
    n_z = n_col // 2
    half = f_in // 2
    pairs = []
    for count in (n_row - 1, n_z - 1, n_z, 1, n_z - 1, n_row - 1, 1, n_z - 1, n_row - 1, 1):
        pairs += [pltpu.SemaphoreType.DMA((count,))] * 2
    act, weight_grad, bias_grad = pl.pallas_call(
        functools.partial(layer, n_row, n_col),
        out_shape=(
            jax.ShapeDtypeStruct((nodes, f_out), BF16),
            jax.ShapeDtypeStruct((f_in, f_out), F32),
            jax.ShapeDtypeStruct((1, f_out), F32),
        ),
        in_specs=[vmem] * 3 + [pl.BlockSpec(memory_space=pl.ANY)] + [vmem] * 4,
        out_specs=(vmem, vmem, vmem),
        scratch_shapes=[
            pltpu.VMEM((slots, block, block), BF16),
            pltpu.VMEM((slots, block, block), BF16),
            pltpu.VMEM((n_col * block, n_row * block), BF16),
            pltpu.VMEM((8, 256), jnp.int32),
            pltpu.VMEM((8, 256), jnp.int32),
            pltpu.SMEM((8, 256), jnp.int32),
            pltpu.SemaphoreType.DMA,
            pltpu.SemaphoreType.DMA,
            pltpu.VMEM((n_row * block, f_in), BF16),
            pltpu.VMEM((n_col, f_in, block), BF16),
            pltpu.VMEM((n_z * block, f_in), BF16),
            pltpu.VMEM((n_z * block, f_in), BF16),
            pltpu.VMEM((n_z * block, f_in), BF16),
            pltpu.VMEM((n_z - 1, block, f_in), BF16),
            pltpu.VMEM((n_row, f_in, block), BF16),
            pltpu.VMEM((n_row - 1, f_in, block), BF16),
            pltpu.VMEM((2, half + 8, f_out), F32),
            pltpu.VMEM((half + 8, f_out), F32),
            pltpu.VMEM((n_z, half + 16, f_out), BF16),
            pltpu.VMEM((n_row, half + 16, f_out), BF16),
            pltpu.VMEM((2, half, f_out), F32),
            *pairs,
        ],
        compiler_params=pltpu.CompilerParams(
            collective_id=0, has_side_effects=True, vmem_limit_bytes=58 * MIB
        ),
        cost_estimate=pl.CostEstimate(
            flops=4 * tiles * block * block * f_in, bytes_accessed=tiles * block * block * 2, transcendentals=0
        ),
        name="layer",
    )(block_rows, block_cols, block_counts, block_values, x_feats, weight, bias, cotangent)
    act, weight_grad, bias_grad = pl.pallas_call(
        finish,
        out_shape=tuple(jax.ShapeDtypeStruct(a.shape, a.dtype) for a in (act, weight_grad, bias_grad)),
        in_specs=[vmem] * 3,
        out_specs=(pl.BlockSpec(memory_space=pl.ANY),) * 3,
        scratch_shapes=[pltpu.SemaphoreType.DMA((3,))],
        name="finish",
    )(act, weight_grad, bias_grad)
    return act, weight_grad, bias_grad.reshape(f_out)


def solution(mesh):
    in_specs = (
        P(("col", "row"), None),
        P(),
        P(),
        P("row", "col", None, None, None),
        P("row", "col", None),
        P("row", "col", None),
        P("row", "col"),
        P(("col", "row"), None),
    )
    out_specs = (P(("col", "row"), None), P(), P())
    return jax.shard_map(
        functools.partial(on_device, mesh.shape["row"], mesh.shape["col"]),
        mesh=mesh, in_specs=in_specs, out_specs=out_specs, check_vma=False,
    )
```

time: 38.3 us -> 29.8 us (0.78)
  local copies, waits for them, and re-layouts: 5.91 us -> 0 us
  Pallas kernels: 30.8 us -> 28.3 us
    unnamed x17 -> x0, local copies, waits for them, and re-layouts: 5.91 us -> none
    pallas_call x1, Pallas kernels: 29.3 us -> 26.8 us  [on_device(): pl.pallas_call(functools.partial(layer, n_row, n_col), out_shape=(jax.Sha...]
where the time goes in v2:
time: 29.8 us; the launch traced here: 29.6 us
  Pallas kernels  28.3 us (95%)
  between operations  1.29 us (4%)
    pallas_call x1, Pallas kernels, on_device(): pl.pallas_call(functools.partial(layer, n_row, n_col), out_shape=(jax.Sha...  26.8 us
    pallas_call x1, Pallas kernels, on_device(): pl.pallas_call(finish, out_shape=tuple((jax.ShapeDtypeStruct(a.shape, a.d...  1.51 us

profile of v2, /device:TPU:0, one launch (start us, length us, event | category | flops | bytes accessed | tf_op | source)
XLA Modules:
  0.0 29.6 jit_solution(2651708137391453977)
XLA Ops:
  1.3 26.8 %layer.1 = (bf16[128,128]{1,0:T(8,128)(2,1)}, f32[128,128]{1,0:T(8,128)}, f32[1,128]{1,0:T(1,128)}) custom-call(s32[1,1,192]{2,1,0:T(1,128)} %rows_ref.1, s32[1,1,192]{2,1,0:T(1,128)} %cols_ref.1, s32[1,1]{1,0:T(1,128)S(6)} %copy.11.count_ref, bf16[1,1,192,128,128]{4,3,2,1,0:T(8,128)(2,1)} %values_ref.1, bf16[128,128]{1,0:T(8,128)(2,1)} %x_ref.1, ...), custom_call_target="tpu_custom_call" | custom-call | flops 268435456 | bytes 1048576 | tf_op jit(solution)/shard_map/layer/pallas_call | solution.py:260
  28.1 1.5 %finish.1 = (bf16[128,128]{1,0:T(8,128)(2,1)}, f32[128,128]{1,0:T(8,128)}, f32[1,128]{1,0:T(1,128)}) custom-call(bf16[128,128]{1,0:T(8,128)(2,1)} %get-tuple-element.9.act_ref, f32[128,128]{1,0:T(8,128)} %get-tuple-element.10.wg_ref, f32[1,128]{1,0:T(1,128)} %get-tuple-element.11.bg_ref), custom_call_target="tpu_custom_call" | custom-call | tf_op jit(solution)/shard_map/finish/pallas_call | solution.py:301

commit v3 on v2

--- a/solution.py
+++ b/solution.py
@@ -22,9 +22,9 @@
 def sort_slots(n_row, n_col, rows_ref, cols_ref, count_ref, keys, order):
     slots = rows_ref.shape[-1]
     log_row = n_row.bit_length() - 1
-    row = jnp.right_shift(rows_ref[0], log_row)
+    row = jnp.right_shift(rows_ref[...], log_row)
     place = jnp.bitwise_and(row, 1) * (n_col // 2) + jnp.right_shift(row, 1)
-    tile = place * n_row + jnp.bitwise_and(cols_ref[0], n_row - 1)
+    tile = place * n_row + jnp.bitwise_and(cols_ref[...], n_row - 1)
     index = lax.broadcasted_iota(jnp.int32, (1, slots), 1)
     tile = jnp.where(index < count_ref[...], tile, n_row * n_col)
     keys[...] = n_row * n_col * 256 + lax.broadcasted_iota(jnp.int32, keys.shape, 1)
@@ -65,15 +65,14 @@
 
 
 def layer(
-    n_row, n_col, rows_ref, cols_ref, count_ref, values_ref, x_ref, w_ref, bias_ref, cot_ref,
+    n_row, n_col, rows_hbm, cols_hbm, count_hbm, values_hbm, x_hbm, w_hbm, bias_hbm, cot_hbm,
     act_ref, wg_ref, bg_ref,
+    rows_ref, cols_ref, count_ref, x_ref, w_ref, bias_ref, cot_ref, input_sems,
     held, runs, tiles_ref, keys, order, order_smem, values_sem, order_sem,
     xcol, xrow, half_out, half_in, sum_out, sum_in, mir_out, mir_in, pair_out, pair_in, over_z, over_row, final,
     s_xrow, r_xrow, s_xz, r_xz, s_xp, r_xp, s_half, r_half, s_sum, r_sum, s_mir, r_mir,
     s_1, r_1, s_2, r_2, s_3, r_3, s_4, r_4,
 ):
-    fetch = pltpu.make_async_copy(values_ref.at[0, 0], held, values_sem)
-    fetch.start()
     r = lax.axis_index("row")
     c = lax.axis_index("col")
     block = x_ref.shape[0]
@@ -98,6 +97,22 @@
         one.start()
         sends.append(one)
 
+    def row_order(t):
+        self_at = lax.rem(2 * r + 1, n_row)
+        t = jnp.where(t < self_at, t, t + 1)
+        return lax.rem(2 * n_row - 1 - r + t, n_row)
+
+    def z_order(t):
+        up = jnp.where(n_z - 1 - t > z, n_z - 1 - t, n_z - 2 - t)
+        down = jnp.where(t < z, t, t + 1)
+        return jnp.where(z < n_z // 2, up, down)
+
+    def row_offset(p):
+        return lax.rem(p - r + n_row, n_row) - 1
+
+    def z_offset(p):
+        return lax.rem(p - z + n_z, n_z) - 1
+
     def row_at(d):
         return lax.rem(r + d, n_row)
 
@@ -110,6 +125,19 @@
     for d in range(1, n_z):
         pl.semaphore_signal(barrier, inc=1, device_id=(r, z_at(d) * 2 + core), device_id_type=MESH)
     pl.semaphore_signal(barrier, inc=1, device_id=mate_id, device_id_type=MESH)
+    inputs = [
+        pltpu.make_async_copy(src, dst, input_sems.at[i])
+        for i, (src, dst) in enumerate((
+            (x_hbm, x_ref), (rows_hbm.at[0], rows_ref), (cols_hbm.at[0], cols_ref), (count_hbm, count_ref),
+            (w_hbm, w_ref), (bias_hbm, bias_ref), (cot_hbm, cot_ref),
+        ))
+    ]
+    for one in inputs:
+        one.start()
+    fetch = pltpu.make_async_copy(values_hbm.at[0, 0], held, values_sem)
+    fetch.start()
+    for one in inputs:
+        one.wait()
     x = x_ref[...]
     xcol[rows_of(r), :] = x
     xrow[here] = x.T
@@ -118,10 +146,13 @@
     to_smem.start()
     pl.semaphore_wait(barrier, n_row + n_z - 1)
 
-    for d in range(1, n_row):
-        send(xcol.at[rows_of(r)], xcol.at[rows_of(r)], s_xrow.at[d - 1], r_xrow.at[d - 1], (row_at(d), c))
-    for d in range(1, n_z):
-        send(xrow.at[here], xrow.at[here], s_xz.at[d - 1], r_xz.at[d - 1], (r, z_at(d) * 2 + core))
+    for t in range(n_z - 1):
+        p = z_order(t)
+        send(xrow.at[here], xrow.at[here], s_xz.at[z_offset(p)], r_xz.at[z_offset(p)], (r, p * 2 + core))
+    for t in range(n_row - 1):
+        p = row_order(t)
+        d = row_offset(p)
+        send(xcol.at[rows_of(r)], xcol.at[rows_of(r)], s_xrow.at[d], r_xrow.at[d], (p, c))
     send(xrow.at[here], xrow.at[here], s_xp.at[0], r_xp.at[0], mate_id)
 
     to_smem.wait()
@@ -148,11 +179,10 @@
     copy(half_out, half_in, s_half.at[0], r_half.at[0], mate_id).wait_recv()
     total = (own + half_in[...].astype(F32)).astype(BF16)
     sum_out[...] = total
-    for d in range(1, n_z):
-        send(
-            sum_out.at[rows_of(z_at(d))], sum_in.at[d - 1], s_sum.at[d - 1], r_sum.at[d - 1],
-            (r, z_at(d) * 2 + core),
-        )
+    for t in range(n_z - 1):
+        p = z_order(t)
+        d = z_offset(p)
+        send(sum_out.at[rows_of(p)], sum_in.at[d], s_sum.at[d], r_sum.at[d], (r, p * 2 + core))
 
     for d in range(n_z):
         slot = xrow.at[mate * n_z + z_at(n_z - d)]
@@ -163,8 +193,10 @@
         both = jnp.dot(xt, tiles_ref[:, 2 * q * block:2 * (q + 1) * block], preferred_element_type=F32).astype(BF16)
         mir_out[2 * q] = both[:, :block]
         mir_out[2 * q + 1] = both[:, block:]
-    for d in range(1, n_row):
-        send(mir_out.at[row_at(d)], mir_in.at[d - 1], s_mir.at[d - 1], r_mir.at[d - 1], (row_at(d), c))
+    for t in range(n_row - 1):
+        p = row_order(t)
+        d = row_offset(p)
+        send(mir_out.at[p], mir_in.at[d], s_mir.at[d], r_mir.at[d], (p, c))
 
     y = sum_out[rows_of(z), :].astype(F32)
     for d in range(1, n_z):
@@ -210,14 +242,16 @@
     copy(pair_in, pair_in, s_1.at[0], r_1.at[0], mate_id).wait_recv()
     both = pair_out[core] + pair_in[...]
     over_z[z] = packed(both[:h, :], both[h:h + 1, :])
-    for d in range(1, n_z):
-        send(over_z.at[z], over_z.at[z], s_2.at[d - 1], r_2.at[d - 1], (r, z_at(d) * 2 + core))
+    for t in range(n_z - 1):
+        p = z_order(t)
+        send(over_z.at[z], over_z.at[z], s_2.at[z_offset(p)], r_2.at[z_offset(p)], (r, p * 2 + core))
     for d in range(1, n_z):
         slot = over_z.at[z_at(n_z - d)]
         copy(slot, slot, s_2.at[d - 1], r_2.at[d - 1], mate_id).wait_recv()
     over_row[r] = packed(*summed(over_z))
-    for d in range(1, n_row):
-        send(over_row.at[r], over_row.at[r], s_3.at[d - 1], r_3.at[d - 1], (row_at(d), c))
+    for t in range(n_row - 1):
+        p = row_order(t)
+        send(over_row.at[r], over_row.at[r], s_3.at[row_offset(p)], r_3.at[row_offset(p)], (p, c))
     for d in range(1, n_row):
         slot = over_row.at[row_at(n_row - d)]
         copy(slot, slot, s_3.at[d - 1], r_3.at[d - 1], mate_id).wait_recv()
@@ -264,9 +298,17 @@
             jax.ShapeDtypeStruct((f_in, f_out), F32),
             jax.ShapeDtypeStruct((1, f_out), F32),
         ),
-        in_specs=[vmem] * 3 + [pl.BlockSpec(memory_space=pl.ANY)] + [vmem] * 4,
+        in_specs=[pl.BlockSpec(memory_space=pltpu.HBM)] * 8,
         out_specs=(vmem, vmem, vmem),
         scratch_shapes=[
+            pltpu.VMEM(block_rows.shape[1:], jnp.int32),
+            pltpu.VMEM(block_cols.shape[1:], jnp.int32),
+            pltpu.VMEM(block_counts.shape, jnp.int32),
+            pltpu.VMEM(x_feats.shape, BF16),
+            pltpu.VMEM(weight.shape, BF16),
+            pltpu.VMEM(bias.shape, F32),
+            pltpu.VMEM(cotangent.shape, BF16),
+            pltpu.SemaphoreType.DMA((7,)),
             pltpu.VMEM((slots, block, block), BF16),
             pltpu.VMEM((slots, block, block), BF16),
             pltpu.VMEM((n_col * block, n_row * block), BF16),

time: 29.8 us -> 29.2 us (0.980)
  Pallas kernels: 28.3 us -> 27.8 us
    pallas_call x1, Pallas kernels: 26.8 us -> 26.3 us  [on_device(): pl.pallas_call(functools.partial(layer, n_row, n_col), out_shape=(jax.Sha...]
where the time goes in v3:
time: 29.2 us; the launch traced here: 29.1 us
  Pallas kernels  27.8 us (95%)
  between operations  1.29 us (4%)
    pallas_call x1, Pallas kernels, on_device(): pl.pallas_call(functools.partial(layer, n_row, n_col), out_shape=(jax.Sha...  26.3 us
    pallas_call x1, Pallas kernels, on_device(): pl.pallas_call(finish, out_shape=tuple((jax.ShapeDtypeStruct(a.shape, a.d...  1.51 us

profile of v3, /device:TPU:0, one launch (start us, length us, event | category | flops | bytes accessed | tf_op | source)
XLA Modules:
  0.0 29.1 jit_solution(10069756629057454966)
XLA Ops:
  1.3 26.3 %layer.1 = (bf16[128,128]{1,0:T(8,128)(2,1)}, f32[128,128]{1,0:T(8,128)}, f32[1,128]{1,0:T(1,128)}) custom-call(s32[1,1,192]{2,1,0:T(1,128)} %rows_hbm.1, s32[1,1,192]{2,1,0:T(1,128)} %cols_hbm.1, s32[1,1]{1,0:T(1,128)S(6)} %copy.11.count_hbm, bf16[1,1,192,128,128]{4,3,2,1,0:T(8,128)(2,1)} %values_hbm.1, bf16[128,128]{1,0:T(8,128)(2,1)} %x_hbm.1, ...), custom_call_target="tpu_custom_call" | custom-call | flops 268435456 | bytes 1048576 | tf_op jit(solution)/shard_map/layer/pallas_call | solution.py:294
  27.6 1.5 %finish.1 = (bf16[128,128]{1,0:T(8,128)(2,1)}, f32[128,128]{1,0:T(8,128)}, f32[1,128]{1,0:T(1,128)}) custom-call(bf16[128,128]{1,0:T(8,128)(2,1)} %get-tuple-element.9.act_ref, f32[128,128]{1,0:T(8,128)} %get-tuple-element.10.wg_ref, f32[1,128]{1,0:T(1,128)} %get-tuple-element.11.bg_ref), custom_call_target="tpu_custom_call" | custom-call | tf_op jit(solution)/shard_map/finish/pallas_call | solution.py:343

commit v4 on v3

--- a/solution.py
+++ b/solution.py
@@ -267,15 +267,10 @@
         one.wait_send()
 
 
-def finish(act_ref, wg_ref, bg_ref, act_out, wg_out, bg_out, sems):
-    copies = [
-        pltpu.make_async_copy(src, dst, sems.at[i])
-        for i, (src, dst) in enumerate(((act_ref, act_out), (wg_ref, wg_out), (bg_ref, bg_out)))
-    ]
-    for one in copies:
-        one.start()
-    for one in copies:
-        one.wait()
+def finish(act_ref, wg_ref, bg_ref, act_out, wg_out, bg_out):
+    act_out[...] = act_ref[...]
+    wg_out[...] = wg_ref[...]
+    bg_out[...] = bg_ref[...]
 
 
 def on_device(n_row, n_col, x_feats, weight, bias, block_values, block_rows, block_cols, block_counts, cotangent):
@@ -344,8 +339,7 @@
         finish,
         out_shape=tuple(jax.ShapeDtypeStruct(a.shape, a.dtype) for a in (act, weight_grad, bias_grad)),
         in_specs=[vmem] * 3,
-        out_specs=(pl.BlockSpec(memory_space=pl.ANY),) * 3,
-        scratch_shapes=[pltpu.SemaphoreType.DMA((3,))],
+        out_specs=(vmem,) * 3,
         name="finish",
     )(act, weight_grad, bias_grad)
     return act, weight_grad, bias_grad.reshape(f_out)

time: 29.2 us -> 29.2 us (level)
  no operation moved by 1% of the time
where the time goes in v4:
time: 29.2 us; the launch traced here: 29 us
  Pallas kernels  27.7 us (95%)
  between operations  1.29 us (4%)
    pallas_call x1, Pallas kernels, on_device(): pl.pallas_call(functools.partial(layer, n_row, n_col), out_shape=(jax.Sha...  26.3 us
    pallas_call x1, Pallas kernels, on_device(): pl.pallas_call(finish, out_shape=tuple((jax.ShapeDtypeStruct(a.shape, a.d...  1.48 us

profile of v4, /device:TPU:0, one launch (start us, length us, event | category | flops | bytes accessed | tf_op | source)
XLA Modules:
  0.0 29.0 jit_solution(8782601428296370852)
XLA Ops:
  1.3 26.3 %layer.1 = (bf16[128,128]{1,0:T(8,128)(2,1)}, f32[128,128]{1,0:T(8,128)}, f32[1,128]{1,0:T(1,128)}) custom-call(s32[1,1,192]{2,1,0:T(1,128)} %rows_hbm.1, s32[1,1,192]{2,1,0:T(1,128)} %cols_hbm.1, s32[1,1]{1,0:T(1,128)S(6)} %copy.11.count_hbm, bf16[1,1,192,128,128]{4,3,2,1,0:T(8,128)(2,1)} %values_hbm.1, bf16[128,128]{1,0:T(8,128)(2,1)} %x_hbm.1, ...), custom_call_target="tpu_custom_call" | custom-call | flops 268435456 | bytes 1048576 | tf_op jit(solution)/shard_map/layer/pallas_call | solution.py:289
  27.6 1.5 %finish.1 = (bf16[128,128]{1,0:T(8,128)(2,1)}, f32[128,128]{1,0:T(8,128)}, f32[1,128]{1,0:T(1,128)}) custom-call(bf16[128,128]{1,0:T(8,128)(2,1)} %get-tuple-element.9.act_ref, f32[128,128]{1,0:T(8,128)} %get-tuple-element.10.wg_ref, f32[1,128]{1,0:T(1,128)} %get-tuple-element.11.bg_ref), custom_call_target="tpu_custom_call" | custom-call | tf_op jit(solution)/shard_map/finish/pallas_call | solution.py:338
